TPU v7x, 512 devices: a whole 4x8x8 slice. The times are simulated.
512 devices in a mesh: pair: 64 (over y_lo, z, core), mo: 8 (over y_hi, x).
Axes of the slice: x: 4, y: 8 (y_hi: 2, y_lo: 4; y = y_hi * 4 + y_lo), z: 8, core: 2. Of those that a mesh axis runs over, the one named last changes fastest.
Arguments:
- packed: bfloat16 [64, 1024, 2048], P(None, 'pair'), may hold values from -6 to 6
- low_diag: bfloat16 [64, 1024], P(None, 'pair'), may hold values from -12 to 12
- occ_coef: bfloat16 [2048, 256], P('pair', 'mo'), may hold values from -0.125 to 0.125
- vir_coef: bfloat16 [2048, 1792], P('pair', 'mo'), may hold values from -0.125 to 0.125
Outputs:
- half_ints: float32 [64, 256, 1792], P('pair', None, 'mo')
All inputs are finite; a program needn't handle non-finite values.
Results may differ from a plain program's by a relative error of at most 0.0029.
Values may be sent and summed in bfloat16 or wider, within the bound.
A program may use at most 64 MiB of HBM per device.

v0:
```python
import jax
import jax.numpy as jnp
from jax import lax
from jax.sharding import PartitionSpec as P


def arrange(coefficient, pair_count, rect_rows):
    basis = coefficient.shape[0]
    half_basis = basis // 2
    columns = coefficient.shape[1]
    upper_part = coefficient[half_basis:].reshape(pair_count, rect_rows, columns)
    lower_part = coefficient[:half_basis][::-1].reshape(pair_count, rect_rows, columns)
    return jnp.stack([upper_part, lower_part], axis=1).reshape(basis, columns)


def shards(packed, low_diag, occ_coef, vir_coef):
    batch_pairs = packed.shape[0]
    rect_rows = packed.shape[1]
    basis = packed.shape[2]
    half_basis = basis // 2
    pair_count = lax.axis_size("pair")
    first_row = lax.axis_index("pair") * rect_rows
    row_index = first_row + lax.broadcasted_iota(jnp.int32, (rect_rows, basis), 0)
    col_index = lax.broadcasted_iota(jnp.int32, (rect_rows, basis), 1)
    hi_pos = half_basis + row_index
    lo_pos = half_basis - 1 - row_index
    hi_rows = jnp.where(col_index < hi_pos, packed, jnp.where(col_index == hi_pos, packed * 0.5, 0))
    flipped = packed[:, :, ::-1]
    lo_rows = jnp.where(
        col_index < lo_pos, flipped, jnp.where(col_index == lo_pos, 0.5 * low_diag[:, :, None], 0)
    )
    lower_rows = jnp.concatenate([hi_rows, lo_rows], axis=1)
    flat_rows = lower_rows.reshape(batch_pairs * 2 * rect_rows, basis)
    vir_panel = lax.all_gather(vir_coef, "pair", axis=0, tiled=True)
    occ_panel = lax.all_gather(occ_coef, "pair", axis=0, tiled=True)
    occ_full = lax.all_gather(occ_panel, "mo", axis=1, tiled=True)
    vir_half = jnp.dot(flat_rows, vir_panel, preferred_element_type=jnp.float32).astype(
        jnp.bfloat16
    )
    vir_half = vir_half.reshape(batch_pairs, 2 * rect_rows, vir_panel.shape[1])
    occ_half = jnp.dot(flat_rows, occ_full, preferred_element_type=jnp.float32).astype(jnp.bfloat16)
    occ_half = occ_half.reshape(batch_pairs, 2 * rect_rows, occ_full.shape[1])
    vir_moved, occ_moved = (
        lax.all_to_all(vir_half, "pair", split_axis=0, concat_axis=1, tiled=True),
        lax.all_to_all(occ_half, "pair", split_axis=0, concat_axis=1, tiled=True),
    )
    occ_arranged = arrange(occ_full, pair_count, rect_rows)
    vir_arranged = arrange(vir_panel, pair_count, rect_rows)
    first_term = jnp.einsum(
        "mi,lma->lia", occ_arranged, vir_moved, preferred_element_type=jnp.float32
    )
    second_term = jnp.einsum(
        "lmi,ma->lia", occ_moved, vir_arranged, preferred_element_type=jnp.float32
    )
    return first_term + second_term


def solution(mesh):
    placed = (P(None, "pair", None), P(None, "pair"), P("pair", "mo"), P("pair", "mo"))
    return jax.shard_map(
        shards, mesh=mesh, in_specs=placed, out_specs=P("pair", None, "mo"), check_vma=False
    )
```

profile of v0, /device:TPU:1, one launch (start us, length us, event | category | flops | bytes accessed | tf_op | source)
XLA Modules:
  0.0 319.6 jit_solution(1507488370429952566)
XLA Ops:
  6.5 88.6 %all_gather.10 = bf16[2048,32]{1,0:T(8,128)(2,1)S(1)} all-gather(bf16[32,32]{1,0:T(8,128)(2,1)} %param.6), channel_id=1, replica_groups=mesh['pair'=64,'mo'=8] {'pair'}, dimensions={0}, use_global_device_ids=true | all-gather | bytes 133120 | tf_op jit(solution)/shard_map/all_gather | solution.py:35
  95.2 0.8 copy.19
  96.3 0.7 broadcast_multiply_fusion
  97.0 11.1 %rev.9 = bf16[64,16,2048]{2,1,0:T(8,128)(2,1)} reverse(bf16[64,16,2048]{2,1,0:T(8,128)(2,1)} %param.4), dimensions={2} | reverse | bytes 8388608 | tf_op jit(solution)/shard_map/rev | solution.py:28
  108.1 4.9 %select_select_fusion.1 = bf16[64,16,2048]{2,1,0:T(8,128)(2,1)} fusion(bf16[64,16,2048]{2,1,0:T(8,128)(2,1)} %param.4, pred[16,2048]{1,0:T(8,128)(4,1)S(1)} %get-tuple-element.10, pred[16,2048]{1,0:T(8,128)(4,1)S(1)} %get-tuple-element.9), kind=kLoop, calls=%fused_computation.2 | loop fusion | flops 6291456 | bytes 8454144 | tf_op jit(solution)/shard_map/jit(_where)/select_n | solution.py:27
  113.1 2.6 select_select_fusion
  115.7 8.4 %pad_maximum_fusion = bf16[64,32,2048]{2,1,0:T(8,128)(2,1)} fusion(bf16[64,16,2048]{2,1,0:T(8,128)(2,1)} %select_select_fusion, bf16[64,16,2048]{2,1,0:T(8,128)(2,1)} %select_select_fusion.1), kind=kLoop, calls=%fused_computation | loop fusion | flops 16777216 | bytes 16777216 | tf_op jit(solution)/shard_map/concatenate | solution.py:32
  124.0 29.0 %all-gather.2.cloned.1.call-done = bf16[2048,256]{0,1:T(8,128)(2,1)} async-done(((bf16[2048,32]{0,1:T(8,128)(2,1)}), bf16[2048,256]{0,1:T(8,128)(2,1)}) %all-gather.2.cloned.1.call-update) | async-done | bytes 1048592 | tf_op jit(solution)/shard_map/all_gather | solution.py:36
  153.0 7.1 %convolution_convert_fusion = bf16[2048,256]{1,0:T(8,128)(2,1)} fusion(bf16[2048,2048]{1,0:T(8,128)(2,1)} %bitcast.31, bf16[2048,256]{0,1:T(8,128)(2,1)} %all-gather.2.cloned.1.call-done), kind=kOutput, calls=%fused_computation.3 | convolution fusion | flops 2148007936 | bytes 10485760 | tf_op jit(solution)/shard_map/dot_general | solution.py:41
  160.1 11.8 %all-to-all-start.1 = ((bf16[64,32,256]{2,1,0:T(8,128)(2,1)}), bf16[64,32,256]{2,1,0:T(8,128)(2,1)S(1)}, u32[]{:S(2)}, u32[]{:S(2)}) async-start(bf16[64,32,256]{2,1,0:T(8,128)(2,1)} %bitcast.8), calls=%async_computation.1 | async-start | bytes 2097152 | tf_op jit(solution)/shard_map/all_to_all | solution.py:45
  172.0 98.0 %all_gather.9 = bf16[2048,224]{1,0:T(8,128)(2,1)S(1)} all-gather(bf16[32,224]{1,0:T(8,128)(2,1)S(1)} %copy-done.1), channel_id=1, replica_groups=mesh['pair'=64,'mo'=8] {'pair'}, dimensions={0}, use_global_device_ids=true | all-gather | bytes 931840 | tf_op jit(solution)/shard_map/all_gather | solution.py:34
  270.0 6.2 %convolution_convert_fusion.1 = bf16[2048,224]{0,1:T(8,128)(2,1)S(1)} fusion(bf16[2048,2048]{1,0:T(8,128)(2,1)} %bitcast.32, bf16[2048,224]{1,0:T(8,128)(2,1)S(1)} %all_gather.9), kind=kOutput, calls=%fused_computation.4 | convolution fusion | flops 1879506944 | bytes 10223616 | tf_op jit(solution)/shard_map/dot_general | solution.py:37
  276.2 1.3 copy.18
  277.5 4.3 %all-to-all-start = ((bf16[64,32,224]{2,1,0:T(8,128)(2,1)}), bf16[64,32,224]{2,1,0:T(8,128)(2,1)S(1)}, u32[]{:S(2)}, u32[]{:S(2)}) async-start(bf16[64,32,224]{2,1,0:T(8,128)(2,1)} %bitcast.37), calls=%async_computation | async-start | bytes 2097152 | tf_op jit(solution)/shard_map/all_to_all | solution.py:44
  281.7 1.1 fusion.4
  282.8 8.3 %rev.11 = bf16[1024,224]{1,0:T(8,128)(2,1)} reverse(bf16[1024,224]{1,0:T(8,128)(2,1)} %get-tuple-element.8), dimensions={0} | reverse | bytes 917504 | tf_op jit(solution)/shard_map/rev | solution.py:12
  291.1 1.4 pad_maximum_fusion.2
  292.5 2.3 fusion.3
  294.7 8.7 %rev.10 = bf16[1024,256]{0,1:T(8,128)(2,1)} reverse(bf16[1024,256]{0,1:T(8,128)(2,1)} %get-tuple-element.6), dimensions={0} | reverse | bytes 1048576 | tf_op jit(solution)/shard_map/rev | solution.py:12
  303.5 2.0 copy.21
  305.5 2.1 copy.20
  307.6 2.3 pad_maximum_fusion.1
  309.9 0.5 convolution_bitcast_fusion
  310.4 2.4 fusion
  (12 shorter events, 0.4 us)
Async XLA Ops:
  6.5 146.5 %all-gather.2.cloned.1.call-start = ((), (), s32[]{:S(2)}) async-start(), calls=%async_computation.2 | async-start | bytes 1179648 | tf_op jit(solution)/shard_map/all_gather | solution.py:36
  108.1 4.9 %copy-start = (bf16[64,16,2048]{2,1,0:T(8,128)(2,1)S(1)}, bf16[64,16,2048]{2,1,0:T(8,128)(2,1)}, u32[]{:S(2)}) copy-start(bf16[64,16,2048]{2,1,0:T(8,128)(2,1)} %rev.9) | copy-start | bytes 12582916
  153.0 18.9 %copy-start.1 = (bf16[32,224]{1,0:T(8,128)(2,1)S(1)}, bf16[32,224]{1,0:T(8,128)(2,1)}, u32[]{:S(2)}) copy-start(bf16[32,224]{1,0:T(8,128)(2,1)} %param.7) | copy-start | bytes 43012
  160.1 117.3 %all-to-all-start.1 = ((bf16[64,32,256]{2,1,0:T(8,128)(2,1)}), bf16[64,32,256]{2,1,0:T(8,128)(2,1)S(1)}, u32[]{:S(2)}, u32[]{:S(2)}) async-start(bf16[64,32,256]{2,1,0:T(8,128)(2,1)} %bitcast.8), calls=%async_computation.1 | async-start | bytes 2097152 | tf_op jit(solution)/shard_map/all_to_all | solution.py:45
  277.5 33.0 %all-to-all-start = ((bf16[64,32,224]{2,1,0:T(8,128)(2,1)}), bf16[64,32,224]{2,1,0:T(8,128)(2,1)S(1)}, u32[]{:S(2)}, u32[]{:S(2)}) async-start(bf16[64,32,224]{2,1,0:T(8,128)(2,1)} %bitcast.37), calls=%async_computation | async-start | bytes 2097152 | tf_op jit(solution)/shard_map/all_to_all | solution.py:44
Sparse Core Ops, SparseCore 0:
  96.2 56.8 all-gather.1
where the time goes:
time: 322 us; the launch traced here: 320 us
  blocking collectives  187 us (58%)
  local copies, waits for them, and re-layouts  37.8 us (12%)
  waiting for transfers between devices  29.1 us (9%)
  other arithmetic  20.4 us (6%)
  matrix products  16.2 us (5%)
  starting transfers between devices  16.1 us (5%)
  between operations  13.5 us (4%)
    all_gather x1, blocking collectives, shards(): vir_panel = lax.all_gather(vir_coef, 'pair', axis=0, tiled=True)  98 us
    all_gather x1, blocking collectives, shards(): occ_panel = lax.all_gather(occ_coef, 'pair', axis=0, tiled=True)  88.6 us
    all_gather x1, waiting for transfers between devices, shards(): occ_full = lax.all_gather(occ_panel, 'mo', axis=1, tiled=True)  29 us
    rev x3, local copies, waits for them, and re-layouts, arrange(): coefficient[:half_basis][::-1].reshape(pair_count, rect_rows, columns)  19.1 us
    all_to_all x1, starting transfers between devices, shards(): lax.all_to_all(occ_half, 'pair', split_axis=0, concat_axis=1, tiled=True)  11.8 us
    rev x1, local copies, waits for them, and re-layouts, shards(): flipped = packed[:, :, ::-1]  11.1 us
    concatenate x1, other arithmetic, shards(): lower_rows = jnp.concatenate([hi_rows, lo_rows], axis=1)  8.37 us
    dot_general x1, matrix products, shards(): jnp.dot(flat_rows, occ_full, preferred_element_type=jnp.float32)  7.08 us
  transfers between devices with their start and end apart: 3, of which 1 were waited for; matrix products, arithmetic and copies ran while one was open for 20% of the time, Pallas kernels for 0%

commit v1 on v0

v1 whole, which is shorter than its diff:
```python
import functools

import jax
import jax.numpy as jnp
from jax import lax
from jax.experimental import pallas as pl
from jax.experimental.pallas import tpu as pltpu
from jax.sharding import PartitionSpec as P

MESH = pl.DeviceIdType.MESH
BF = jnp.bfloat16
F32 = jnp.float32
YL, YH, NX, NC = 4, 2, 4, 2
YR = YL * YH


def iota(shape, dim):
    return lax.broadcasted_iota(jnp.int32, shape, dim)


def anti_identity(n):
    return (iota((n, n), 0) + iota((n, n), 1) == n - 1).astype(BF)


def kernel(
    pairs, mos, packed, low_diag, occ, vir, out,
    raw, slab, part, p_occ, p_vir, pan, xo, rp_send, rp, acc,
    raw_s, raw_r, slab_s, part_s, part_r, oz_s, oz_r, oy_s, oy_r, oc_s, oc_r,
    vz_s, vz_r, vy_s, vy_r, vc_s, vc_r, rp_s, rp_r, xo_s, xo_r,
):
    nz = pairs // (YL * NC)
    per = pairs // mos
    chunk = 16 * per
    half = pairs * 16
    nocc = occ.shape[1] * mos
    nvir = vir.shape[1]
    p, m = lax.axis_index("pair"), lax.axis_index("mo")
    ylo, z, core = p // (nz * NC), lax.rem(p // NC, nz), lax.rem(p, NC)
    yhi, x = m // NX, lax.rem(m, NX)
    y = yhi * YL + ylo

    def pair_at(y_, z_, c_):
        return (lax.rem(y_, YL) * nz + z_) * NC + c_

    def to(q, k):
        return {"pair": q, "mo": k}

    def along_y(step):
        y_ = lax.rem(y + step + YR, YR)
        return to(pair_at(y_, z, core), (y_ // YL) * NX + x)

    def remote(src, dst, s, r, dev):
        return pltpu.make_async_remote_copy(
            src_ref=src, dst_ref=dst, send_sem=s, recv_sem=r, device_id=dev, device_id_type=MESH
        )

    def take(ref, sem):
        pltpu.make_async_copy(ref, ref, sem).wait()

    barrier = pltpu.get_barrier_semaphore()

    def greet(dev):
        pl.semaphore_signal(barrier, inc=1, device_id=dev, device_id_type=MESH)

    @pl.loop(1, pairs)
    def _(q):
        greet(to(lax.rem(p + q, pairs), m))

    @pl.loop(1, mos)
    def _(q):
        greet(to(p, lax.rem(m + q, mos)))

    for step in (1, -1, 2, -2):
        greet(along_y(step))

    @pl.loop(0, per)
    def _(j):
        @pl.when((m * per + j != p) | (p // per != m))
        def _():
            greet(to(m * per + j, p // per))

    slab_copy = pltpu.make_async_copy(packed.at[pl.ds(m * per, per)], slab, slab_s.at[0])
    slab_copy.start()
    turn = jnp.where(
        p < pairs // 2,
        (iota((32, 32), 0) + iota((32, 32), 1) == 31).astype(F32),
        (iota((32, 32), 0) == iota((32, 32), 1)).astype(F32),
    ).astype(BF)
    spread = (iota((nvir, 256), 0) == iota((nvir, 256), 1)).astype(BF)
    vir_turned = jnp.dot(turn, vir[...], preferred_element_type=F32).astype(BF)
    p_vir[ylo, core, z] = jnp.dot(vir_turned, spread, preferred_element_type=F32).astype(BF)
    spread = (iota((occ.shape[1], 128), 0) == iota((occ.shape[1], 128), 1)).astype(BF)
    part[m] = jnp.dot(occ[...], spread, preferred_element_type=F32).astype(BF)

    pl.semaphore_wait(barrier, pairs - 1 + mos - 1 + 4 + per - (p // per == m).astype(jnp.int32))

    @pl.loop(1, mos)
    def _(q):
        remote(part.at[m], part.at[m], part_s, part_r, to(p, lax.rem(m + q, mos))).start()

    @pl.loop(1, nz)
    def _(q):
        slot = p_vir.at[ylo, core, z]
        remote(slot, slot, vz_s, vz_r, to(pair_at(ylo, lax.rem(z + q, nz), core), m)).start()

    starts = (half - chunk * (m + 1), half + chunk * m)

    def send_raw(side):
        cols = pl.ds(pl.multiple_of(starts[side], 128) if chunk % 128 == 0 else starts[side], chunk)
        rows = pl.ds(pl.multiple_of(p * 16, 16), 16)
        pltpu.make_async_copy(packed.at[p, :, cols], raw.at[side, rows], slab_s.at[1 + side]).start()

        @pl.loop(1, pairs)
        def _(q):
            dest = lax.rem(p + q, pairs)
            remote(
                packed.at[dest, :, cols], raw.at[side, rows], raw_s.at[side], raw_r.at[side], to(dest, m)
            ).start()

    send_raw(0)

    take(part.at[pl.ds(0, mos - 1)], part_r)
    block = jnp.zeros((32, nocc), F32)
    for k in range(mos):
        place = (iota((128, nocc), 0) + k * occ.shape[1] == iota((128, nocc), 1)) & (
            iota((128, nocc), 0) < occ.shape[1]
        )
        block += jnp.dot(part[k], place.astype(BF), preferred_element_type=F32)
    p_occ[ylo, core, z] = jnp.dot(turn, block.astype(BF), preferred_element_type=F32).astype(BF)

    @pl.loop(1, nz)
    def _(q):
        slot = p_occ.at[ylo, core, z]
        remote(slot, slot, oz_s, oz_r, to(pair_at(ylo, lax.rem(z + q, nz), core), m)).start()

    send_raw(1)

    sibling = to(pair_at(ylo, z, 1 - core), m)
    take(p_occ.at[0, 0, pl.ds(0, nz - 1)], oz_r)
    mine = p_occ.at[ylo, core]
    remote(mine, mine, oy_s.at[0], oy_r.at[0], along_y(1)).start()
    remote(mine, mine, oy_s.at[1], oy_r.at[1], along_y(-1)).start()
    remote(mine, mine, oy_s.at[2], oy_r.at[2], along_y(2 - 4 * core)).start()
    remote(mine, mine, oc_s.at[0], oc_r.at[0], sibling).start()

    take(p_vir.at[0, 0, pl.ds(0, nz - 1)], vz_r)

    def pass_vir(s, up, down):
        held = p_vir.at[s, core]

        def go(up_way):
            step = 1 if up_way else -1
            remote(
                held, held, vy_s.at[s, int(up_way)], vy_r.at[s], to(pair_at(ylo + step, z, core), m)
            ).start()

        if up:
            pl.when(ylo < YL - 1)(lambda: go(True))
        if down:
            pl.when(ylo > 0)(lambda: go(False))
        remote(held, held, vc_s.at[s], vc_r.at[s], sibling).start()

    pass_vir(ylo, True, True)

    for k, step in enumerate((-1, 1, 2)):
        theirs = p_occ.at[lax.rem(ylo + step + YL, YL), core]
        take(theirs, oy_r.at[k])
        remote(theirs, theirs, oc_s.at[k + 1], oc_r.at[k + 1], sibling).start()
    for k, step in enumerate((0, -1, 1, 2)):
        take(p_occ.at[lax.rem(ylo + step + YL, YL), 1 - core], oc_r.at[k])

    def blocks_of(k):
        firsts = [pairs // 2 + k * (chunk // 32) + b for b in range(chunk // 32)]
        for q in firsts + [pairs - 1 - q for q in firsts]:
            yield q // (nz * NC), q % NC, q // NC % nz

    for k in range(mos):
        for b, at in enumerate(blocks_of(k)):
            pan[k, b * 32 : (b + 1) * 32] = p_occ[at]

    flip = anti_identity(chunk)
    nothing = jnp.zeros((chunk, chunk), BF)
    slab_copy.wait()
    diag = jnp.sum(
        jnp.where(
            iota((mos, per, 16), 0) == m, low_diag[...].astype(F32).reshape(mos, per, 16), 0.0
        ),
        axis=0,
    )
    diag = jnp.sum(
        jnp.where(
            iota((per, 16, 16), 1) == iota((per, 16, 16), 2),
            jnp.broadcast_to(diag[:, None, :], (per, 16, 16)),
            0.0,
        ),
        axis=2,
        keepdims=True,
    )
    diag = jnp.broadcast_to(diag, (per, 16, chunk)).reshape(chunk, chunk)
    row = p * 16 + lax.rem(iota((chunk, chunk), 0), 16)
    rows_sum = jnp.zeros((2 * chunk, nocc), F32)
    for k in range(mos):
        a = slab[:, :, half + k * chunk : half + (k + 1) * chunk].reshape(chunk, chunk).astype(F32)
        b = slab[:, :, half - (k + 1) * chunk : half - k * chunk].reshape(chunk, chunk)
        b = jnp.dot(b, flip, preferred_element_type=F32).astype(BF)
        col = k * chunk + iota((chunk, chunk), 1)
        a_low = jnp.where(col < row, a, jnp.where(col == row, a * 0.5, 0.0)).astype(BF)
        a_up = jnp.where(col > row, a, jnp.where(col == row, diag, 0.0)).astype(BF)
        left = jnp.concatenate(
            [jnp.concatenate([a_low, b], axis=1), jnp.concatenate([nothing, a_up], axis=1)], axis=0
        )
        rows_sum += jnp.dot(left, pan[k], preferred_element_type=F32)
    rows_sum = rows_sum.astype(BF)
    rp_send[:, 0:16] = rows_sum[:chunk].reshape(per, 16, nocc)
    rp_send[:, 16:32] = rows_sum[chunk:].reshape(per, 16, nocc)

    own_row = lax.rem(p, per)

    @pl.loop(0, per)
    def _(j):
        dst = rp.at[own_row]

        @pl.when((m * per + j == p) & (p // per == m))
        def _():
            pltpu.make_async_copy(rp_send.at[j], dst, rp_r.at[j]).start()

        @pl.when((m * per + j != p) | (p // per != m))
        def _():
            remote(rp_send.at[j], dst, rp_s.at[j], rp_r.at[own_row], to(m * per + j, p // per)).start()

    for d in range(1, YL):
        for sign in (-1, 1):
            s = ylo + sign * d

            @pl.when((s >= 0) & (s < YL))
            def _(s=s, sign=sign):
                take(p_vir.at[s, core], vy_r.at[s])
                pass_vir(s, sign < 0, sign > 0)

    rest = pl.ds(0, (pairs - 1) * 16)
    for side in range(2):
        pltpu.make_async_copy(raw.at[side, pl.ds(0, 16)], raw.at[side, pl.ds(0, 16)], slab_s.at[1 + side]).wait()
        take(raw.at[side, rest], raw_r.at[side])
    total = jnp.zeros((nocc, 2 * chunk), F32)
    for k in range(mos):
        here = slice(k * chunk, (k + 1) * chunk)
        a = raw[1, here].astype(F32)
        b = jnp.dot(raw[0, here], flip, preferred_element_type=F32).astype(BF)
        row = k * chunk + iota((chunk, chunk), 0)
        col = m * chunk + iota((chunk, chunk), 1)
        a_low = jnp.where(col < row, a, jnp.where(col == row, a * 0.5, 0.0)).astype(BF)
        a_up = jnp.where(col > row, a, 0.0).astype(BF)
        right = jnp.concatenate(
            [jnp.concatenate([a_low, b], axis=1), jnp.concatenate([nothing, a_up], axis=1)], axis=0
        )
        total += lax.dot_general(pan[k], right, (((0,), (0,)), ((), ())), preferred_element_type=F32)

    for j in range(per):
        take(rp.at[j], rp_r.at[j])
    hi_rows = rp[:, 0:16].reshape(chunk, nocc).astype(F32)
    lo_rows = rp[:, 16:32].reshape(chunk, nocc).astype(F32)
    total += jnp.concatenate([hi_rows, lo_rows], axis=0).T
    xo[m] = total.astype(BF)

    other = (1 - yhi) * NX

    def round_x(step):
        return to(p, yhi * NX + lax.rem(x + step + NX, NX))

    def slot_of(base, step):
        return xo.at[base + lax.rem(x + step + NX, NX)]

    own, twin = xo.at[m], xo.at[other + x]
    base = yhi * NX
    remote(own, own, xo_s.at[0], xo_r.at[0], to(p, other + x)).start()
    remote(own, own, xo_s.at[1], xo_r.at[1], round_x(1)).start()
    remote(own, own, xo_s.at[2], xo_r.at[2], round_x(-1)).start()

    for s in range(YL):
        take(p_vir.at[s, 1 - core], vc_r.at[s])
    for k in range(mos):
        for b, at in enumerate(blocks_of(k)):
            pan[k, b * 32 : (b + 1) * 32, 0:256] = p_vir[at]

    def add(at):
        acc[...] += jnp.dot(xo[at], pan[at], preferred_element_type=F32)

    acc[...] = jnp.dot(xo[m], pan[m], preferred_element_type=F32)
    take(slot_of(base, -1), xo_r.at[1])
    fwd = slot_of(base, -1)
    remote(fwd, fwd, xo_s.at[3], xo_r.at[3], round_x(1)).start()
    take(twin, xo_r.at[0])
    remote(twin, twin, xo_s.at[4], xo_r.at[4], round_x(1)).start()
    remote(twin, twin, xo_s.at[5], xo_r.at[5], round_x(-1)).start()
    add(base + lax.rem(x + NX - 1, NX))
    add(other + x)
    take(slot_of(base, 1), xo_r.at[2])
    add(base + lax.rem(x + 1, NX))
    take(slot_of(other, 1), xo_r.at[5])
    fwd = slot_of(other, 1)
    remote(fwd, fwd, xo_s.at[6], xo_r.at[6], round_x(-1)).start()
    add(other + lax.rem(x + 1, NX))
    take(slot_of(base, 2), xo_r.at[3])
    add(base + lax.rem(x + 2, NX))
    take(slot_of(other, -1), xo_r.at[4])
    add(other + lax.rem(x + NX - 1, NX))
    take(slot_of(other, 2), xo_r.at[6])
    add(other + lax.rem(x + 2, NX))
    out[0] = acc[:, :nvir]

    take(part.at[pl.ds(0, mos - 1)], part_s)
    take(p_vir.at[0, 0, pl.ds(0, nz - 1)], vz_s)
    take(p_occ.at[0, 0, pl.ds(0, nz - 1)], oz_s)
    for side in range(2):
        take(raw.at[side, rest], raw_s.at[side])
    for k in range(3):
        take(p_occ.at[0, 0], oy_s.at[k])
    for k in range(4):
        take(p_occ.at[0, 0], oc_s.at[k])
        take(p_vir.at[0, 0], vc_s.at[k])

    for s in range(YL):
        @pl.when((s <= ylo) & (ylo < YL - 1))
        def _(s=s):
            take(p_vir.at[0, 0], vy_s.at[s, 1])

        @pl.when((s >= ylo) & (ylo > 0))
        def _(s=s):
            take(p_vir.at[0, 0], vy_s.at[s, 0])

    @pl.loop(0, per)
    def _(j):
        @pl.when((m * per + j != p) | (p // per != m))
        def _():
            take(rp_send.at[j], rp_s.at[j])

    for k in range(7):
        take(xo.at[0], xo_s.at[k])


def shards(pairs, mos, packed, low_diag, occ_coef, vir_coef):
    per = pairs // mos
    chunk = 16 * per
    nz = pairs // (YL * NC)
    nocc = occ_coef.shape[1] * mos
    nvir = vir_coef.shape[1]
    dma = pltpu.SemaphoreType.DMA
    one = dma(())
    vmem = pl.BlockSpec(memory_space=pltpu.VMEM)
    return pl.pallas_call(
        functools.partial(kernel, pairs, mos),
        out_shape=jax.ShapeDtypeStruct((1, nocc, nvir), F32),
        in_specs=[pl.BlockSpec(memory_space=pltpu.HBM), vmem, vmem, vmem],
        out_specs=vmem,
        scratch_shapes=[
            pltpu.VMEM((2, 16 * pairs, chunk), BF),
            pltpu.VMEM((per, 16, packed.shape[2]), BF),
            pltpu.VMEM((mos, 32, 128), BF),
            pltpu.VMEM((YL, NC, nz, 32, nocc), BF),
            pltpu.VMEM((YL, NC, nz, 32, 256), BF),
            pltpu.VMEM((mos, 2 * chunk, 256), BF),
            pltpu.VMEM((mos, nocc, 2 * chunk), BF),
            pltpu.VMEM((per, 32, nocc), BF),
            pltpu.VMEM((per, 32, nocc), BF),
            pltpu.VMEM((nocc, 256), F32),
            dma((2,)), dma((2,)), dma((3,)), one, one, one, one, dma((3,)), dma((3,)),
            dma((4,)), dma((4,)), one, one, dma((YL, 2)), dma((YL,)), dma((YL,)), dma((YL,)),
            dma((per,)), dma((per,)), dma((7,)), dma((7,)),
        ],
        compiler_params=pltpu.CompilerParams(
            collective_id=0, has_side_effects=True, vmem_limit_bytes=40 * 1024 * 1024
        ),
    )(packed, low_diag, occ_coef, vir_coef)


def solution(mesh):
    sizes = dict(mesh.shape)
    placed = (P(None, "pair", None), P(None, "pair"), P("pair", "mo"), P("pair", "mo"))
    return jax.shard_map(
        functools.partial(shards, sizes["pair"], sizes["mo"]),
        mesh=mesh, in_specs=placed, out_specs=P("pair", None, "mo"), check_vma=False,
    )
```

time: 322 us -> 82.8 us (0.26)
  the two profiles are of different devices: /device:TPU:1 before, /device:TPU:2 now
where the time goes in v1:
time: 82.8 us; the launch traced here: 82.5 us
  Pallas kernels  77.3 us (93%)
  local copies, waits for them, and re-layouts  5.19 us (6%)
    pallas_call x1, Pallas kernels, shards(): pl.pallas_call(functools.partial(kernel, pairs, mos), out_shape=jax.Shape...  77.3 us
    unnamed x7, local copies, waits for them, and re-layouts  4.38 us

profile of v1, /device:TPU:2, one launch (start us, length us, event | category | flops | bytes accessed | tf_op | source)
XLA Modules:
  0.0 82.5 jit_solution(5199118415137535566)
XLA Ops:
  0.0 0.8 copy.5.low_diag
  0.8 0.0 copy-start
  0.8 2.2 %copy-done = bf16[64,16,2048]{2,1,0:T(8,128)(2,1)S(1)} copy-done((bf16[64,16,2048]{2,1,0:T(8,128)(2,1)S(1)}, bf16[64,16,2048]{2,1,0:T(8,128)(2,1)}, u32[]{:S(2)}) %copy-start) | copy-done | bytes 4194328
  3.0 0.0 copy-start.1
  3.0 0.7 copy-done.1
  3.7 0.0 copy-start.2
  3.7 0.7 copy-done.2
  4.4 77.3 %shard_map.46 = f32[1,256,224]{2,1,0:T(8,128)S(1)} custom-call(bf16[64,16,2048]{2,1,0:T(8,128)(2,1)S(1)} %copy-done, bf16[64,16]{1,0:T(8,128)(2,1)S(1)} %copy.5.low_diag, bf16[32,32]{1,0:T(8,128)(2,1)S(1)} %copy-done.2, bf16[32,224]{1,0:T(8,128)(2,1)S(1)} %copy-done.1), custom_call_target="tpu_custom_call" | custom-call | tf_op jit(solution)/shard_map/pallas_call | solution.py:350
  81.7 0.8 copy.6
Async XLA Ops:
  0.8 2.2 %copy-start = (bf16[64,16,2048]{2,1,0:T(8,128)(2,1)S(1)}, bf16[64,16,2048]{2,1,0:T(8,128)(2,1)}, u32[]{:S(2)}) copy-start(bf16[64,16,2048]{2,1,0:T(8,128)(2,1)} %packed.1) | copy-start | bytes 12582916
  3.0 0.7 copy-start.1
  3.7 0.7 copy-start.2

commit v2 on v0

v2 whole, which is shorter than its diff:
```python
import functools

import jax
import jax.numpy as jnp
from jax import lax
from jax.experimental import pallas as pl
from jax.experimental.pallas import tpu as pltpu
from jax.sharding import PartitionSpec as P

MESH = pl.DeviceIdType.MESH
BF = jnp.bfloat16
F32 = jnp.float32
YL, YH, NX, NC = 4, 2, 4, 2
YR = YL * YH
SCHED = (
    ("vy", 0),
    ("r101", 0),
    ("r001", 2),
    ("vz0", 2),
    ("vz1", 4),
    ("vz2", 5),
    ("vz3", 6),
    ("vz4", 8),
)


def iota(shape, dim):
    return lax.broadcasted_iota(jnp.int32, shape, dim)


def kernel(
    pairs, mos, packed, low_diag_in, occ_in, vir_in, out,
    raw, slab, part, p_occ, p_vir, left, xo, rp_send, rp, acc, occ, vir, low_diag,
    in_s, raw_s, raw_r, raw_l, part_s, part_r, oz_s, oz_r, oy_s, oy_r, oc_s, oc_r,
    vy_s, vy_r, vz_s, vz_r, vc_s, vc_r, rp_s, rp_r, xo_s, xo_r,
):
    nz = pairs // (YL * NC)
    per = pairs // mos
    chunk = 16 * per
    half = pairs * 16
    nocc = occ.shape[1] * mos
    nvir = vir.shape[1]
    p, m = lax.axis_index("pair"), lax.axis_index("mo")

    def place(q):
        return q // (nz * NC), lax.rem(q // NC, nz), lax.rem(q, NC)

    ylo, z, core = place(p)
    yhi, x = m // NX, lax.rem(m, NX)
    y = yhi * YL + ylo

    def pair_at(y_, z_, c_):
        return (lax.rem(y_, YL) * nz + z_) * NC + c_

    def to(q, k):
        return {"pair": q, "mo": k}

    def mo_of(y_):
        return (lax.rem(y_ + YR, YR) // YL) * NX + x

    def along_y(step):
        return to(pair_at(lax.rem(y + step + YR, YR), z, core), mo_of(y + step))

    def shift(q):
        y_, z_, c_ = place(q)
        return lax.rem(z_ + 2 * y_ + c_, mos)

    def block_of(q, k):
        return lax.rem(k + shift(q), mos)

    mine = block_of(p, m)

    def remote(src, dst, s, r, dev):
        return pltpu.make_async_remote_copy(
            src_ref=src, dst_ref=dst, send_sem=s, recv_sem=r, device_id=dev, device_id_type=MESH
        )

    def take(ref, sem):
        pltpu.make_async_copy(ref, ref, sem).wait()

    turnover = lax.rem(p // per - m + mos, mos)

    def target(j):
        y_, c_ = j // NC, lax.rem(j, NC)
        return pair_at(y_, lax.rem(turnover - 2 * y_ - c_ + 2 * mos, mos), c_)

    own_row = lax.rem(p, per)
    keeps = mine == p // per

    def nearest(q, z_even_up):
        d = lax.rem(q // (nz * NC) - ylo + YL, YL)
        far = jnp.where(z_even_up, 2, -2)
        return jnp.where(d == 3, -1, jnp.where(d == 2, far, d))

    slab_copies = [
        pltpu.make_async_copy(packed.at[target(j)], slab.at[j], in_s.at[j]) for j in range(per)
    ]
    small_copies = [
        pltpu.make_async_copy(occ_in, occ, in_s.at[per]),
        pltpu.make_async_copy(vir_in, vir, in_s.at[per + 1]),
        pltpu.make_async_copy(low_diag_in, low_diag, in_s.at[per + 2]),
    ]
    for copy in small_copies + slab_copies:
        copy.start()

    barrier = pltpu.get_barrier_semaphore()

    def greet(dev):
        pl.semaphore_signal(barrier, inc=1, device_id=dev, device_id_type=MESH)

    @pl.loop(1, mos)
    def _(q):
        greet(to(p, lax.rem(m + q, mos)))

    for step in (1, -1, 2, -2):
        greet(along_y(step))

    @pl.loop(1, YL)
    def _(q):
        greet(to(pair_at(ylo + q, z, core), m))

    @pl.loop(1, pairs)
    def _(q):
        source = lax.rem(p + q, pairs)
        even = lax.rem(source // NC, 2) == 0
        greet(to(source, mo_of(y + nearest(source, jnp.logical_not(even)))))

    @pl.loop(0, per)
    def _(j):
        @pl.when(mine * per + j != p)
        def _():
            greet(to(mine * per + j, m))

    for copy in small_copies:
        copy.wait()
    turn = jnp.where(
        p < pairs // 2,
        (iota((32, 32), 0) + iota((32, 32), 1) == 31).astype(F32),
        (iota((32, 32), 0) == iota((32, 32), 1)).astype(F32),
    ).astype(BF)
    spread = (iota((occ.shape[1], 128), 0) == iota((occ.shape[1], 128), 1)).astype(BF)
    part[m] = jnp.dot(occ[...], spread, preferred_element_type=F32).astype(BF)
    spread = (iota((nvir, 256), 0) == iota((nvir, 256), 1)).astype(BF)
    vir_turned = jnp.dot(turn, vir[...], preferred_element_type=F32).astype(BF)
    p_vir[core, z, ylo] = jnp.dot(vir_turned, spread, preferred_element_type=F32).astype(BF)

    pl.semaphore_wait(barrier, pairs - 1 + mos - 1 + 4 + YL - 1 + per - keeps.astype(jnp.int32))

    @pl.loop(1, mos)
    def _(q):
        remote(part.at[m], part.at[m], part_s, part_r, to(p, lax.rem(m + q, mos))).start()

    rows = pl.ds(pl.multiple_of(p * 16, 16), 16)

    def columns(side, b):
        first = half + chunk * b if side else half - chunk * (b + 1)
        return pl.ds(pl.multiple_of(first, 128), chunk)

    for side in range(2):
        pltpu.make_async_copy(
            packed.at[p, :, columns(side, mine)], raw.at[side, rows], raw_l.at[side]
        ).start()

    def send_raw(side, lo, hi):
        even = lax.rem(z, 2) == 0

        @pl.loop(lo, hi)
        def _(q):
            dest = lax.rem(p + q, pairs)
            k = mo_of(y + nearest(dest, even))
            remote(
                packed.at[dest, :, columns(side, block_of(dest, k))], raw.at[side, rows],
                raw_s.at[side], raw_r.at[side], to(dest, k),
            ).start()

    sibling = to(pair_at(ylo, z, 1 - core), m)

    def vir_over_y():
        @pl.loop(1, YL)
        def _(q):
            slot = p_vir.at[core, z, ylo]
            remote(slot, slot, vy_s, vy_r, to(pair_at(ylo + q, z, core), m)).start()

    def vir_on(d, ways):
        for way in range(2) if d else range(1):
            sign = 1 - 2 * way
            group = p_vir.at[core, lax.rem(z - sign * d + nz, nz)]

            def go(way, sign):
                remote(
                    group, group, vz_s.at[d + 1, way], vz_r.at[d + 1, way],
                    to(pair_at(ylo, lax.rem(z + sign + nz, nz), core), m),
                ).start()

            def handle():
                if d:
                    take(group, vz_r.at[d, way])
                if d == 0:
                    go(0, 1)
                    go(1, -1)
                elif d < nz // 2 - 1:
                    go(way, sign)
                elif d == nz // 2 - 1:
                    pl.when(core == way)(lambda: go(way, sign))
                remote(group, group, vc_s, vc_r, sibling).start()

            if d == nz // 2:
                pl.when(core == way)(handle)
            else:
                handle()

    def run(action):
        if action[0] == "r":
            side, part_, parts_ = int(action[1]), int(action[2]), int(action[3])
            send_raw(side, max(1, pairs * part_ // parts_), pairs * (part_ + 1) // parts_)
        elif action == "vy":
            vir_over_y()
        elif action == "vz0":
            take(p_vir.at[0, 0, pl.ds(0, YL - 1)], vy_r)
            vir_on(0, 1)
        else:
            vir_on(int(action[2:]), 2)

    def point(n):
        for action, at in SCHED:
            if at == n:
                run(action)

    point(0)

    take(part.at[pl.ds(0, mos - 1)], part_r)
    block = jnp.zeros((32, nocc), F32)
    for k in range(mos):
        at = (iota((128, nocc), 0) + k * occ.shape[1] == iota((128, nocc), 1)) & (
            iota((128, nocc), 0) < occ.shape[1]
        )
        block += jnp.dot(part[k], at.astype(BF), preferred_element_type=F32)
    p_occ[ylo, core, z] = jnp.dot(turn, block.astype(BF), preferred_element_type=F32).astype(BF)

    order = [1, nz - 1, 2, nz - 2, 3, nz - 3, nz // 2]
    ways_y = (1, -1, 2 - 4 * core)

    def occ_on(q, g):
        got = p_occ.at[ylo, core, lax.rem(z - q + nz, nz)]
        if q:
            take(got, oz_r.at[q])
        for k, step in enumerate(ways_y):
            remote(got, got, oy_s.at[k, g], oy_r.at[k, g], along_y(step)).start()
        remote(got, got, oc_s.at[0, g], oc_r.at[0, g], sibling).start()

    own = p_occ.at[ylo, core, z]
    for q in order:
        remote(own, own, oz_s, oz_r.at[q], to(pair_at(ylo, lax.rem(z + q, nz), core), m)).start()
    occ_on(0, 0)
    point(1)
    for i, q in enumerate(order):
        occ_on(q, int(i >= nz // 2 - 1))
    point(2)

    for copy in slab_copies:
        copy.wait()
    flip = (iota((chunk, chunk), 0) + iota((chunk, chunk), 1) == chunk - 1).astype(BF)
    nothing = jnp.zeros((chunk, chunk), BF)
    diag = jnp.concatenate(
        [
            jnp.sum(
                jnp.where(iota((16, pairs), 1) == target(j), low_diag[...].astype(F32), 0.0),
                axis=1, keepdims=True,
            )
            for j in range(per)
        ],
        axis=0,
    )
    row = p * 16 + lax.rem(iota((chunk, chunk), 0), 16)
    for k in range(mos):
        a = slab[:, :, half + k * chunk : half + (k + 1) * chunk].reshape(chunk, chunk).astype(F32)
        b = slab[:, :, half - (k + 1) * chunk : half - k * chunk].reshape(chunk, chunk)
        b = jnp.dot(b, flip, preferred_element_type=F32).astype(BF)
        col = k * chunk + iota((chunk, chunk), 1)
        a_low = jnp.where(col < row, a, jnp.where(col == row, a * 0.5, 0.0)).astype(BF)
        a_up = jnp.where(col > row, a, jnp.where(col == row, diag, 0.0)).astype(BF)
        left[k] = jnp.concatenate(
            [jnp.concatenate([a_low, b], axis=1), jnp.concatenate([nothing, a_up], axis=1)], axis=0
        )

    far_blocks = [order[i] for i in range(nz // 2 - 1, nz - 1)]
    near_blocks = [0] + [order[i] for i in range(nz // 2 - 1)]
    for g, qs in enumerate((near_blocks, far_blocks)):
        for k, step in enumerate((-1, 1, 2)):
            s_ = lax.rem(ylo + step + YL, YL)
            take(p_occ.at[0, 0, pl.ds(0, len(qs))], oy_r.at[k, g])
            for q in qs:
                theirs = p_occ.at[s_, core, lax.rem(z - q + nz, nz)]
                remote(theirs, theirs, oc_s.at[k + 1, g], oc_r.at[k + 1, g], sibling).start()
    for g, qs in enumerate((near_blocks, far_blocks)):
        for k in range(4):
            take(p_occ.at[0, 0, pl.ds(0, len(qs))], oc_r.at[k, g])
    point(3)

    def blocks_of(k):
        firsts = [pairs // 2 + k * (chunk // 32) + b for b in range(chunk // 32)]
        for q in firsts + [pairs - 1 - q for q in firsts]:
            yield q // (nz * NC), q % NC, q // NC % nz

    def pan(k):
        return jnp.concatenate([p_occ[at] for at in blocks_of(k)], axis=0)

    rows_sum = jnp.zeros((2 * chunk, nocc), F32)
    for k in range(mos):
        rows_sum += jnp.dot(left[k], pan(k), preferred_element_type=F32)
    rows_sum = rows_sum.astype(BF)
    rp_send[:, 0:16] = rows_sum[:chunk].reshape(per, 16, nocc)
    rp_send[:, 16:32] = rows_sum[chunk:].reshape(per, 16, nocc)

    @pl.loop(0, per)
    def _(j):
        dst = rp.at[own_row]

        @pl.when(target(j) == p)
        def _():
            pltpu.make_async_copy(rp_send.at[j], dst, rp_r.at[own_row]).start()

        @pl.when(target(j) != p)
        def _():
            remote(rp_send.at[j], dst, rp_s.at[j], rp_r.at[own_row], to(target(j), m)).start()

    point(4)

    rest = pl.ds(0, (pairs - 1) * 16)

    def wait_raw(side):
        one = raw.at[side, pl.ds(0, 16)]
        pltpu.make_async_copy(one, one, raw_l.at[side]).wait()
        take(raw.at[side, rest], raw_r.at[side])

    def trans_dot(a, b):
        return lax.dot_general(a, b, (((0,), (0,)), ((), ())), preferred_element_type=F32)

    wait_raw(1)
    col = mine * chunk + iota((chunk, chunk), 1)
    hi_sum = jnp.zeros((chunk, nocc), F32)
    for k in range(mos):
        a = raw[1, k * chunk : (k + 1) * chunk].astype(F32)
        row = k * chunk + iota((chunk, chunk), 0)
        a_low = jnp.where(col < row, a, jnp.where(col == row, a * 0.5, 0.0)).astype(BF)
        hi_sum += trans_dot(a_low, pan(k)[:chunk])
    wait_raw(0)
    lo_sum = jnp.zeros((chunk, nocc), F32)
    for k in range(mos):
        here = slice(k * chunk, (k + 1) * chunk)
        a = raw[1, here].astype(F32)
        b = jnp.dot(raw[0, here], flip, preferred_element_type=F32).astype(BF)
        row = k * chunk + iota((chunk, chunk), 0)
        a_up = jnp.where(col > row, a, 0.0).astype(BF)
        lo_sum += trans_dot(jnp.concatenate([b, a_up], axis=0), pan(k))

    other, base = (1 - yhi) * NX, yhi * NX

    def round_x(step):
        return to(p, base + lax.rem(x + step + NX, NX))

    def slot(h, first, step):
        return xo.at[first + lax.rem(x + step + NX, NX), h]

    def send_xo(h, which, ref, dev):
        remote(ref, ref, xo_s.at[h, which], xo_r.at[h, which], dev).start()

    def got_xo(h, which, ref):
        take(ref, xo_r.at[h, which])

    point(5)
    for j in range(per):
        take(rp.at[j], rp_r.at[j])
    for h, column_sum in enumerate((hi_sum, lo_sum)):
        row_sum = rp[:, 16 * h : 16 * h + 16].reshape(chunk, nocc).astype(F32)
        xo[m, h] = (column_sum + row_sum).astype(BF)
        send_xo(h, 0, xo.at[m, h], to(p, other + x))
        send_xo(h, 1, xo.at[m, h], round_x(1))
        send_xo(h, 2, xo.at[m, h], round_x(-1))

    point(6)
    for h in range(2):
        got_xo(h, 1, slot(h, base, -1))
        send_xo(h, 3, slot(h, base, -1), round_x(1))
    point(7)
    for h in range(2):
        twin = xo.at[other + x, h]
        got_xo(h, 0, twin)
        send_xo(h, 4, twin, round_x(1))
        send_xo(h, 5, twin, round_x(-1))
    point(8)

    take(p_vir.at[1 - core], vc_r)
    for k in range(mos):
        left[k] = jnp.concatenate([p_vir[c, z_, y_] for y_, c, z_ in blocks_of(k)], axis=0)

    def add(h, first, step, fresh=False):
        at = first + lax.rem(x + step + NX, NX)
        term = trans_dot(left[block_of(p, at), h * chunk : (h + 1) * chunk], xo[at, h])
        acc[...] = term if fresh else acc[...] + term

    for h in range(2):
        add(h, base, 0, fresh=h == 0)
        add(h, base, -1)
        add(h, other, 0)
    for h in range(2):
        got_xo(h, 2, slot(h, base, 1))
        add(h, base, 1)
        got_xo(h, 5, slot(h, other, 1))
        send_xo(h, 6, slot(h, other, 1), round_x(-1))
        add(h, other, 1)
    for h in range(2):
        got_xo(h, 3, slot(h, base, 2))
        add(h, base, 2)
        got_xo(h, 4, slot(h, other, -1))
        add(h, other, -1)
    for h in range(2):
        got_xo(h, 6, slot(h, other, 2))
        add(h, other, 2)
    out[0] = acc[:nvir]

    take(part.at[pl.ds(0, mos - 1)], part_s)
    take(p_occ.at[0, 0, pl.ds(0, nz - 1)], oz_s)
    for side in range(2):
        take(raw.at[side, rest], raw_s.at[side])
    for g, qs in enumerate((near_blocks, far_blocks)):
        for k in range(3):
            take(p_occ.at[0, 0, pl.ds(0, len(qs))], oy_s.at[k, g])
        for k in range(4):
            take(p_occ.at[0, 0, pl.ds(0, len(qs))], oc_s.at[k, g])
    take(p_vir.at[0, 0, pl.ds(0, YL - 1)], vy_s)
    for d in range(1, nz // 2):
        for way in range(2):
            take(p_vir.at[0, 0], vz_s.at[d, way])
    for way in range(2):
        pl.when(core == way)(lambda way=way: take(p_vir.at[0, 0], vz_s.at[nz // 2, way]))
    take(p_vir.at[core], vc_s)

    @pl.loop(0, per)
    def _(j):
        @pl.when(target(j) != p)
        def _():
            take(rp_send.at[j], rp_s.at[j])

    for h in range(2):
        for k in range(7):
            take(xo.at[0, 0], xo_s.at[h, k])


def shards(pairs, mos, packed, low_diag, occ_coef, vir_coef):
    per = pairs // mos
    chunk = 16 * per
    nz = pairs // (YL * NC)
    nocc = occ_coef.shape[1] * mos
    nvir = vir_coef.shape[1]
    dma = pltpu.SemaphoreType.DMA
    one = dma(())
    hbm = pl.BlockSpec(memory_space=pltpu.HBM)
    return pl.pallas_call(
        functools.partial(kernel, pairs, mos),
        out_shape=jax.ShapeDtypeStruct((1, nvir, nocc), F32),
        in_specs=[hbm] * 4,
        out_specs=pl.BlockSpec(memory_space=pltpu.VMEM),
        scratch_shapes=[
            pltpu.VMEM((2, 16 * pairs, chunk), BF),
            pltpu.VMEM((per, 16, packed.shape[2]), BF),
            pltpu.VMEM((mos, 32, 128), BF),
            pltpu.VMEM((YL, NC, nz, 32, nocc), BF),
            pltpu.VMEM((NC, nz, YL, 32, 256), BF),
            pltpu.VMEM((mos, 2 * chunk, 2 * chunk), BF),
            pltpu.VMEM((mos, 2, chunk, nocc), BF),
            pltpu.VMEM((per, 32, nocc), BF),
            pltpu.VMEM((per, 32, nocc), BF),
            pltpu.VMEM((256, nocc), F32),
            pltpu.VMEM(occ_coef.shape, BF),
            pltpu.VMEM(vir_coef.shape, BF),
            pltpu.VMEM((16, pairs), BF),
            dma((per + 3,)), dma((2,)), dma((2,)), dma((2,)), one, one,
            one, dma((nz,)), dma((3, 2)), dma((3, 2)), dma((4, 2)), dma((4, 2)),
            one, one, dma((nz // 2 + 1, 2)), dma((nz // 2 + 1, 2)), one, one,
            dma((per,)), dma((per,)), dma((2, 7)), dma((2, 7)),
        ],
        compiler_params=pltpu.CompilerParams(
            collective_id=0, has_side_effects=True, vmem_limit_bytes=62 * 1024 * 1024
        ),
    )(packed, low_diag.T, occ_coef, vir_coef).transpose(0, 2, 1)


def solution(mesh):
    sizes = dict(mesh.shape)
    placed = (P(None, "pair", None), P(None, "pair"), P("pair", "mo"), P("pair", "mo"))
    return jax.shard_map(
        functools.partial(shards, sizes["pair"], sizes["mo"]),
        mesh=mesh, in_specs=placed, out_specs=P("pair", None, "mo"), check_vma=False,
    )
```

time: 322 us -> 65.4 us (0.20)
  blocking collectives: 187 us -> 0 us
  Pallas kernels: 0 us -> 63.7 us
  local copies, waits for them, and re-layouts: 37.8 us -> 1.64 us
  waiting for transfers between devices: 29.1 us -> 0 us
  other arithmetic: 20.4 us -> 0 us
  matrix products: 16.2 us -> 0 us
  starting transfers between devices: 16.1 us -> 0 us
  between operations: 13.5 us -> 0.01 us
    all_gather x2 -> x0, blocking collectives: 187 us -> none  [the longest x1 98 us: shards(): vir_panel = lax.all_gather(vir_coef, 'pair', axis=0, tiled=True)]
    pallas_call x0 -> x1, Pallas kernels: none -> 63.7 us  [shards(): pl.pallas_call(functools.partial(kernel, pairs, mos), out_shape=jax.Shape...]
    rev x4 -> x0, local copies, waits for them, and re-layouts: 30.1 us -> none  [the longest x3 19.1 us: arrange(): coefficient[:half_basis][::-1].reshape(pair_count, rect_rows, columns)]
    all_gather x1 -> x0, waiting for transfers between devices: 29 us -> none  [shards(): occ_full = lax.all_gather(occ_panel, 'mo', axis=1, tiled=True)]
    dot_general x4 -> x0, matrix products: 16.2 us -> none  [the longest x1 7.08 us: shards(): jnp.dot(flat_rows, occ_full, preferred_element_type=jnp.float32)]
    all_to_all x2 -> x0, starting transfers between devices: 16.1 us -> none  [the longest x1 11.8 us: shards(): lax.all_to_all(occ_half, 'pair', split_axis=0, concat_axis=1, tiled=True)]
    concatenate x1 -> x0, other arithmetic: 8.37 us -> none  [shards(): lower_rows = jnp.concatenate([hi_rows, lo_rows], axis=1)]
    select_n x2 -> x0, other arithmetic: 7.51 us -> none  [the longest x1 4.92 us: shards(): jnp.where(col_index < hi_pos, packed, jnp.where(col_index == hi_pos, pack...]
  transfers between devices with their start and end apart: 3 -> 0, of which waited for: 1 -> 0; matrix products, arithmetic and copies ran while one was open for 20% -> 0% of each run, Pallas kernels for 0% -> 0%
where the time goes in v2:
time: 65.4 us; the launch traced here: 65.3 us
  Pallas kernels  63.7 us (97%)
  local copies, waits for them, and re-layouts  1.64 us (3%)
    pallas_call x1, Pallas kernels, shards(): pl.pallas_call(functools.partial(kernel, pairs, mos), out_shape=jax.Shape...  63.7 us
    unnamed x1, local copies, waits for them, and re-layouts  1.64 us

profile of v2, /device:TPU:1, one launch (start us, length us, event | category | flops | bytes accessed | tf_op | source)
XLA Modules:
  0.0 65.3 jit_solution(7307870085633954603)
XLA Ops:
  0.0 63.7 %shard_map.46 = f32[1,224,256]{2,1,0:T(8,128)} custom-call(bf16[64,16,2048]{2,1,0:T(8,128)(2,1)} %packed.1, bf16[16,64]{1,0:T(8,128)(2,1)} %bitcast.3, bf16[32,32]{1,0:T(8,128)(2,1)} %occ_in.1, bf16[32,224]{1,0:T(8,128)(2,1)} %vir_in.1), custom_call_target="tpu_custom_call" | custom-call | tf_op jit(solution)/shard_map/pallas_call | solution.py:459
  63.7 1.6 %copy.6 = f32[1,256,224]{1,2,0:T(8,128)} copy(f32[1,256,224]{1,2,0:T(8,128)} %bitcast.2) | data formatting | bytes 458752

commit v3 on v2

v3 whole, which is shorter than its diff:
```python
import functools

import jax
import jax.numpy as jnp
from jax import lax
from jax.experimental import pallas as pl
from jax.experimental.pallas import tpu as pltpu
from jax.sharding import PartitionSpec as P

MESH = pl.DeviceIdType.MESH
BF = jnp.bfloat16
F32 = jnp.float32
YL, YH, NX, NC = 4, 2, 4, 2
YR = YL * YH
SCHED = (
    ("vy", 0),
    ("r101", 0),
    ("r001", 2),
    ("vz0", 4),
    ("vz1", 6),
    ("vz2", 8),
)
NP = 2


def iota(shape, dim):
    return lax.broadcasted_iota(jnp.int32, shape, dim)


def kernel(
    pairs, mos, packed, low_diag_in, occ_in, vir_in, out,
    raw, slab, part, p_occ, p_vir, left, right, xo, rp_send, rp, acc, occ, vir, low_diag,
    in_s, raw_s, raw_r, raw_l, part_s, part_r, oz_s, oz_r, oy_s, oy_r, oc_s, oc_r,
    vy_s, vy_r, vz_s, vz_r, vc_s, vc_r, rp_s, rp_r, xo_s, xo_r,
):
    nz = pairs // (YL * NC)
    per = pairs // mos
    chunk = 16 * per
    half = pairs * 16
    nocc = occ.shape[1] * mos
    nvir = vir.shape[1]
    p, m = lax.axis_index("pair"), lax.axis_index("mo")

    def place(q):
        return q // (nz * NC), lax.rem(q // NC, nz), lax.rem(q, NC)

    ylo, z, core = place(p)
    yhi, x = m // NX, lax.rem(m, NX)
    y = yhi * YL + ylo

    def pair_at(y_, z_, c_):
        return (lax.rem(y_, YL) * nz + z_) * NC + c_

    def to(q, k):
        return {"pair": q, "mo": k}

    def mo_of(y_):
        return (lax.rem(y_ + YR, YR) // YL) * NX + x

    def along_y(step):
        return to(pair_at(lax.rem(y + step + YR, YR), z, core), mo_of(y + step))

    def shift(q):
        y_, z_, c_ = place(q)
        return lax.rem(z_ + 2 * y_ + c_, mos)

    def block_of(q, k):
        return lax.rem(k + shift(q), mos)

    mine = block_of(p, m)

    def remote(src, dst, s, r, dev):
        return pltpu.make_async_remote_copy(
            src_ref=src, dst_ref=dst, send_sem=s, recv_sem=r, device_id=dev, device_id_type=MESH
        )

    def take(ref, sem):
        pltpu.make_async_copy(ref, ref, sem).wait()

    turnover = lax.rem(p // per - m + mos, mos)

    def target(j):
        y_, c_ = j // NC, lax.rem(j, NC)
        return pair_at(y_, lax.rem(turnover - 2 * y_ - c_ + 2 * mos, mos), c_)

    own_row = lax.rem(p, per)
    keeps = mine == p // per

    def nearest(q, z_even_up):
        d = lax.rem(q // (nz * NC) - ylo + YL, YL)
        far = jnp.where(z_even_up, 2, -2)
        return jnp.where(d == 3, -1, jnp.where(d == 2, far, d))

    slab_copies = [
        pltpu.make_async_copy(packed.at[target(j)], slab.at[j], in_s.at[j]) for j in range(per)
    ]
    small_copies = [
        pltpu.make_async_copy(occ_in, occ, in_s.at[per]),
        pltpu.make_async_copy(vir_in, vir, in_s.at[per + 1]),
        pltpu.make_async_copy(low_diag_in, low_diag, in_s.at[per + 2]),
    ]
    for copy in small_copies + slab_copies:
        copy.start()

    barrier = pltpu.get_barrier_semaphore()

    def greet(dev):
        pl.semaphore_signal(barrier, inc=1, device_id=dev, device_id_type=MESH)

    @pl.loop(1, mos)
    def _(q):
        greet(to(p, lax.rem(m + q, mos)))

    for step in (1, -1, 2, -2):
        greet(along_y(step))

    @pl.loop(1, YL)
    def _(q):
        greet(to(pair_at(ylo + q, z, core), m))

    @pl.loop(1, pairs)
    def _(q):
        source = lax.rem(p + q, pairs)
        even = lax.rem(source // NC, 2) == 0
        greet(to(source, mo_of(y + nearest(source, jnp.logical_not(even)))))

    @pl.loop(0, per)
    def _(j):
        @pl.when(mine * per + j != p)
        def _():
            greet(to(mine * per + j, m))

    for copy in small_copies:
        copy.wait()
    turn = jnp.where(
        p < pairs // 2,
        (iota((32, 32), 0) + iota((32, 32), 1) == 31).astype(F32),
        (iota((32, 32), 0) == iota((32, 32), 1)).astype(F32),
    ).astype(BF)
    wide = occ.shape[1]
    part[m] = sum(
        jnp.dot(
            occ[16 * i : 16 * i + 16],
            (iota((wide, 128), 0) + wide * i == iota((wide, 128), 1)).astype(BF),
            preferred_element_type=F32,
        )
        for i in range(2)
    ).astype(BF)
    spread = (iota((nvir, 256), 0) == iota((nvir, 256), 1)).astype(BF)
    vir_turned = jnp.dot(turn, vir[...], preferred_element_type=F32).astype(BF)
    p_vir[core, z, ylo] = jnp.dot(vir_turned, spread, preferred_element_type=F32).astype(BF)

    pl.semaphore_wait(barrier, pairs - 1 + mos - 1 + 4 + YL - 1 + per - keeps.astype(jnp.int32))

    @pl.loop(1, mos)
    def _(q):
        remote(part.at[m], part.at[m], part_s, part_r, to(p, lax.rem(m + q, mos))).start()

    rows = pl.ds(pl.multiple_of(p * 16, 16), 16)

    def columns(side, b):
        first = half + chunk * b if side else half - chunk * (b + 1)
        return pl.ds(pl.multiple_of(first, 128), chunk)

    for side in range(2):
        pltpu.make_async_copy(
            packed.at[p, :, columns(side, mine)], raw.at[side, rows], raw_l.at[side]
        ).start()

    def send_raw(side, lo, hi):
        even = lax.rem(z, 2) == 0

        @pl.loop(lo, hi)
        def _(q):
            dest = lax.rem(p + q * 23, pairs)
            k = mo_of(y + nearest(dest, even))
            remote(
                packed.at[dest, :, columns(side, block_of(dest, k))], raw.at[side, rows],
                raw_s.at[side], raw_r.at[side], to(dest, k),
            ).start()

    sibling = to(pair_at(ylo, z, 1 - core), m)

    def vir_over_y():
        @pl.loop(1, YL)
        def _(q):
            slot = p_vir.at[core, z, ylo]
            remote(slot, slot, vy_s, vy_r, to(pair_at(ylo + q, z, core), m)).start()

    def group(step):
        return p_vir.at[core, lax.rem(z + step + nz, nz)]

    def vir_to(held, i, step):
        dev = to(pair_at(ylo, lax.rem(z + step + nz, nz), core), m)
        remote(held, held, vz_s.at[i], vz_r.at[i], dev).start()

    def vir_to_sibling(held):
        remote(held, held, vc_s, vc_r, sibling).start()

    def vir_near():
        take(p_vir.at[0, 0, pl.ds(0, YL - 1)], vy_r)
        for i, step in enumerate((1, -1, 2, -2)):
            vir_to(group(0), i, step)
        vir_to_sibling(group(0))

    def vir_far():
        for i, step in ((2, 1), (3, -1)):
            held = group(-2 * step)
            take(held, vz_r.at[i])
            vir_to(held, i + 2, step)
            pl.when(core == i - 2)(lambda held=held, step=step: vir_to(held, 6, 2 * step))
            vir_to_sibling(held)
        for i, step in ((0, 1), (1, -1)):
            take(group(-step), vz_r.at[i])
            vir_to_sibling(group(-step))

    def vir_last():
        for i, step in ((4, -3), (5, 3), (6, 4)):
            take(group(step), vz_r.at[i])
            vir_to_sibling(group(step))

    def run(action):
        if action[0] == "r":
            side, part_, parts_ = int(action[1]), int(action[2]), int(action[3])
            send_raw(side, max(1, pairs * part_ // parts_), pairs * (part_ + 1) // parts_)
        elif action == "vy":
            vir_over_y()
        elif action == "vz0":
            vir_near()
        elif action == "vz1":
            vir_far()
        else:
            vir_last()

    def point(n):
        for action, at in SCHED:
            if at == n:
                run(action)

    point(0)

    take(part.at[pl.ds(0, mos - 1)], part_r)
    pair_rows = jnp.zeros((16, 2 * nocc), F32)
    lane, col = iota((128, 2 * nocc), 0), iota((128, 2 * nocc), 1)
    for k in range(mos):
        at = ((lane < wide) & (col == k * wide + lane)) | (
            (lane >= wide) & (lane < 2 * wide) & (col == nocc + (k - 1) * wide + lane)
        )
        pair_rows += jnp.dot(part[k], at.astype(BF), preferred_element_type=F32)
    block = jnp.concatenate([pair_rows[:, :nocc], pair_rows[:, nocc:]], axis=0).astype(BF)
    block = jnp.dot(turn, block, preferred_element_type=F32).astype(BF)
    ncol = nocc // NP
    for h in range(NP):
        p_occ[h, ylo, core, z] = block[:, h * ncol : (h + 1) * ncol]

    order = [1, nz - 1, 2, nz - 2, 3, nz - 3, nz // 2]
    ways_y = (1, -1, 2 - 4 * core)

    def occ_on(h, q):
        got = p_occ.at[h, ylo, core, lax.rem(z - q + nz, nz)]
        if q:
            take(got, oz_r.at[h, q])
        for k, step in enumerate(ways_y):
            remote(got, got, oy_s.at[h, k], oy_r.at[h, k], along_y(step)).start()

    for h in range(NP):
        own = p_occ.at[h, ylo, core, z]
        for q in order:
            remote(
                own, own, oz_s, oz_r.at[h, q], to(pair_at(ylo, lax.rem(z + q, nz), core), m)
            ).start()
        occ_on(h, 0)
    point(1)
    for h in range(NP):
        for q in order:
            occ_on(h, q)
        held = p_occ.at[h, ylo, core]
        remote(held, held, oc_s.at[h, 0], oc_r.at[h, 0], sibling).start()
    point(2)

    for copy in slab_copies:
        copy.wait()
    flip = (iota((chunk, chunk), 0) + iota((chunk, chunk), 1) == chunk - 1).astype(BF)
    nothing = jnp.zeros((chunk, chunk), BF)
    diag = jnp.concatenate(
        [
            jnp.sum(
                jnp.where(iota((16, pairs), 1) == target(j), low_diag[...].astype(F32), 0.0),
                axis=1, keepdims=True,
            )
            for j in range(per)
        ],
        axis=0,
    )
    row = p * 16 + lax.rem(iota((chunk, chunk), 0), 16)
    for k in range(mos):
        a = slab[:, :, half + k * chunk : half + (k + 1) * chunk].reshape(chunk, chunk).astype(F32)
        b = slab[:, :, half - (k + 1) * chunk : half - k * chunk].reshape(chunk, chunk)
        b = jnp.dot(b, flip, preferred_element_type=F32).astype(BF)
        col = k * chunk + iota((chunk, chunk), 1)
        a_low = jnp.where(col < row, a, jnp.where(col == row, a * 0.5, 0.0)).astype(BF)
        a_up = jnp.where(col > row, a, jnp.where(col == row, diag, 0.0)).astype(BF)
        left[k] = jnp.concatenate(
            [jnp.concatenate([a_low, b], axis=1), jnp.concatenate([nothing, a_up], axis=1)], axis=0
        )

    def occ_to_sibling(h):
        for k, step in enumerate((-1, 1, 2)):
            theirs = p_occ.at[h, lax.rem(ylo + step + YL, YL), core]
            take(theirs, oy_r.at[h, k])
            remote(theirs, theirs, oc_s.at[h, k + 1], oc_r.at[h, k + 1], sibling).start()
        for k in range(4):
            take(p_occ.at[0, 0, 0], oc_r.at[h, k])

    def blocks_of(k):
        firsts = [pairs // 2 + k * (chunk // 32) + b for b in range(chunk // 32)]
        for q in firsts + [pairs - 1 - q for q in firsts]:
            yield q // (nz * NC), q % NC, q // NC % nz

    def occ_rows(h, k):
        return jnp.concatenate([p_occ[(h, *at)] for at in blocks_of(k)], axis=0)

    def row_part(h):
        rows_sum = jnp.zeros((2 * chunk, ncol), F32)
        for k in range(mos):
            rows_sum += jnp.dot(left[k], occ_rows(h, k), preferred_element_type=F32)
        rows_sum = rows_sum.astype(BF)
        rp_send[h, :, 0:16] = rows_sum[:chunk].reshape(per, 16, ncol)
        rp_send[h, :, 16:32] = rows_sum[chunk:].reshape(per, 16, ncol)

        @pl.loop(0, per)
        def _(j):
            dst = rp.at[h, own_row]

            @pl.when(target(j) == p)
            def _():
                pltpu.make_async_copy(rp_send.at[h, j], dst, rp_r.at[h, own_row]).start()

            @pl.when(target(j) != p)
            def _():
                remote(
                    rp_send.at[h, j], dst, rp_s.at[h, j], rp_r.at[h, own_row], to(target(j), m)
                ).start()

    for h in range(NP):
        occ_to_sibling(h)
        row_part(h)
        point(3 + h)

    rest = pl.ds(0, (pairs - 1) * 16)
    for side in range(2):
        one = raw.at[side, pl.ds(0, 16)]
        pltpu.make_async_copy(one, one, raw_l.at[side]).wait()
        take(raw.at[side, rest], raw_r.at[side])

    def by_rows(a, b):
        return lax.dot_general(a, b, (((1,), (1,)), ((), ())), preferred_element_type=F32)

    same = (iota((chunk, chunk), 0) == iota((chunk, chunk), 1)).astype(BF)
    here = mine * chunk + iota((chunk, chunk), 0)
    for k in range(mos):
        rows_k = slice(k * chunk, (k + 1) * chunk)
        there = k * chunk + iota((chunk, chunk), 1)
        a = by_rows(same, raw[1, rows_k])
        a_low = jnp.where(here < there, a, jnp.where(here == there, a * 0.5, 0.0)).astype(BF)
        a_up = jnp.where(here > there, a, 0.0).astype(BF)
        b = by_rows(flip, raw[0, rows_k]).astype(BF)
        right[k] = jnp.concatenate(
            [jnp.concatenate([a_low, nothing], axis=1), jnp.concatenate([b, a_up], axis=1)], axis=0
        )
    column_sums = []
    for h in range(NP):
        column_sum = jnp.zeros((2 * chunk, ncol), F32)
        for k in range(mos):
            column_sum += jnp.dot(right[k], occ_rows(h, k), preferred_element_type=F32)
        column_sums.append(column_sum)

    other, base = (1 - yhi) * NX, yhi * NX

    def round_x(step):
        return to(p, base + lax.rem(x + step + NX, NX))

    def slot(h, first, step):
        return xo.at[first + lax.rem(x + step + NX, NX), h]

    def send_xo(h, which, ref, dev):
        remote(ref, ref, xo_s.at[h, which], xo_r.at[h, which], dev).start()

    def got_xo(h, which, ref):
        take(ref, xo_r.at[h, which])

    point(5)
    for h in range(NP):
        for j in range(per):
            take(rp.at[h, j], rp_r.at[h, j])
        row_sum = jnp.concatenate(
            [rp[h, :, 0:16].reshape(chunk, ncol), rp[h, :, 16:32].reshape(chunk, ncol)], axis=0
        )
        xo[m, h] = (column_sums[h] + row_sum.astype(F32)).astype(BF)
        send_xo(h, 0, xo.at[m, h], to(p, other + x))
        send_xo(h, 1, xo.at[m, h], round_x(1))
        send_xo(h, 2, xo.at[m, h], round_x(-1))

    point(6)
    for h in range(NP):
        got_xo(h, 1, slot(h, base, -1))
        send_xo(h, 3, slot(h, base, -1), round_x(1))
    point(7)
    for h in range(NP):
        twin = xo.at[other + x, h]
        got_xo(h, 0, twin)
        send_xo(h, 4, twin, round_x(1))
        send_xo(h, 5, twin, round_x(-1))
        send_xo(h, 6, twin, round_x(2))
    point(8)

    take(p_vir.at[1 - core], vc_r)
    unit = (iota((256, 256), 0) == iota((256, 256), 1)).astype(BF)
    for k in range(mos):
        rows_k = jnp.concatenate([p_vir[c, z_, y_] for y_, c, z_ in blocks_of(k)], axis=0)
        left[k] = by_rows(unit, rows_k).astype(BF)

    def add(h, first, step, fresh=False):
        at = first + lax.rem(x + step + NX, NX)
        term = jnp.dot(left[block_of(p, at)], xo[at, h], preferred_element_type=F32)
        acc[h] = term if fresh else acc[h] + term

    for h in range(NP):
        add(h, base, 0, fresh=True)
        add(h, base, -1)
        add(h, other, 0)
    for h in range(NP):
        got_xo(h, 2, slot(h, base, 1))
        add(h, base, 1)
        got_xo(h, 5, slot(h, other, 1))
        add(h, other, 1)
    for h in range(NP):
        got_xo(h, 3, slot(h, base, 2))
        add(h, base, 2)
        got_xo(h, 4, slot(h, other, -1))
        add(h, other, -1)
    for h in range(NP):
        got_xo(h, 6, slot(h, other, 2))
        add(h, other, 2)
    out[0] = jnp.concatenate([acc[h, :nvir] for h in range(NP)], axis=1)

    take(part.at[pl.ds(0, mos - 1)], part_s)
    for h in range(NP):
        for k in range(3):
            take(p_occ.at[0, 0, 0], oy_s.at[h, k])
        for k in range(4):
            take(p_occ.at[0, 0, 0], oc_s.at[h, k])
    take(p_occ.at[:, 0, 0, pl.ds(0, nz - 1)], oz_s)
    for side in range(2):
        take(raw.at[side, rest], raw_s.at[side])
    take(p_vir.at[0, 0, pl.ds(0, YL - 1)], vy_s)
    for i in range(7):
        take(p_vir.at[0, 0], vz_s.at[i])
    take(p_vir.at[core], vc_s)

    @pl.loop(0, per)
    def _(j):
        @pl.when(target(j) != p)
        def _():
            for h in range(NP):
                take(rp_send.at[h, j], rp_s.at[h, j])

    for h in range(NP):
        for k in range(7):
            take(xo.at[0, 0], xo_s.at[h, k])


def shards(pairs, mos, packed, low_diag, occ_coef, vir_coef):
    per = pairs // mos
    chunk = 16 * per
    nz = pairs // (YL * NC)
    nocc = occ_coef.shape[1] * mos
    nvir = vir_coef.shape[1]
    dma = pltpu.SemaphoreType.DMA
    one = dma(())
    hbm = pl.BlockSpec(memory_space=pltpu.HBM)
    return pl.pallas_call(
        functools.partial(kernel, pairs, mos),
        out_shape=jax.ShapeDtypeStruct((1, nvir, nocc), F32),
        in_specs=[hbm] * 4,
        out_specs=pl.BlockSpec(memory_space=pltpu.VMEM),
        scratch_shapes=[
            pltpu.VMEM((2, 16 * pairs, chunk), BF),
            pltpu.VMEM((per, 16, packed.shape[2]), BF),
            pltpu.VMEM((mos, 16, 128), BF),
            pltpu.VMEM((NP, YL, NC, nz, 32, nocc // NP), BF),
            pltpu.VMEM((NC, nz, YL, 32, 256), BF),
            pltpu.VMEM((mos, 2 * chunk, 2 * chunk), BF),
            pltpu.VMEM((mos, 2 * chunk, 2 * chunk), BF),
            pltpu.VMEM((mos, NP, 2 * chunk, nocc // NP), BF),
            pltpu.VMEM((NP, per, 32, nocc // NP), BF),
            pltpu.VMEM((NP, per, 32, nocc // NP), BF),
            pltpu.VMEM((NP, 256, nocc // NP), F32),
            pltpu.VMEM(occ_coef.shape, BF),
            pltpu.VMEM(vir_coef.shape, BF),
            pltpu.VMEM((16, pairs), BF),
            dma((per + 3,)), dma((2,)), dma((2,)), dma((2,)), one, one,
            one, dma((NP, nz)), dma((NP, 3)), dma((NP, 3)), dma((NP, 4)), dma((NP, 4)),
            one, one, dma((7,)), dma((7,)), one, one,
            dma((NP, per)), dma((NP, per)), dma((NP, 7)), dma((NP, 7)),
        ],
        compiler_params=pltpu.CompilerParams(
            collective_id=0, has_side_effects=True, vmem_limit_bytes=62 * 1024 * 1024
        ),
    )(packed, low_diag.T, occ_coef, vir_coef).transpose(0, 2, 1)


def solution(mesh):
    sizes = dict(mesh.shape)
    placed = (P(None, "pair", None), P(None, "pair"), P("pair", "mo"), P("pair", "mo"))
    return jax.shard_map(
        functools.partial(shards, sizes["pair"], sizes["mo"]),
        mesh=mesh, in_specs=placed, out_specs=P("pair", None, "mo"), check_vma=False,
    )
```

time: 65.4 us -> 61.8 us (0.945)
  Pallas kernels: 63.7 us -> 60 us
    pallas_call x1, Pallas kernels: 63.7 us -> 60 us  [shards(): pl.pallas_call(functools.partial(kernel, pairs, mos), out_shape=jax.Shape...]
where the time goes in v3:
time: 61.8 us; the launch traced here: 61.7 us
  Pallas kernels  60 us (97%)
  local copies, waits for them, and re-layouts  1.64 us (3%)
    pallas_call x1, Pallas kernels, shards(): pl.pallas_call(functools.partial(kernel, pairs, mos), out_shape=jax.Shape...  60 us
    unnamed x1, local copies, waits for them, and re-layouts  1.64 us

profile of v3, /device:TPU:1, one launch (start us, length us, event | category | flops | bytes accessed | tf_op | source)
XLA Modules:
  0.0 61.7 jit_solution(10936241681017377142)
XLA Ops:
  0.0 60.0 %shard_map.46 = f32[1,224,256]{2,1,0:T(8,128)} custom-call(bf16[64,16,2048]{2,1,0:T(8,128)(2,1)} %packed.1, bf16[16,64]{1,0:T(8,128)(2,1)} %bitcast.3, bf16[32,32]{1,0:T(8,128)(2,1)} %occ_in.1, bf16[32,224]{1,0:T(8,128)(2,1)} %vir_in.1), custom_call_target="tpu_custom_call" | custom-call | tf_op jit(solution)/shard_map/pallas_call | solution.py:482
  60.0 1.6 %copy.6 = f32[1,256,224]{1,2,0:T(8,128)} copy(f32[1,256,224]{1,2,0:T(8,128)} %bitcast.2) | data formatting | bytes 458752

commit v4 on v3

--- a/solution.py
+++ b/solution.py
@@ -16,7 +16,7 @@
     ("vy", 0),
     ("r101", 0),
     ("r001", 2),
-    ("vz0", 4),
+    ("vz0", 3),
     ("vz1", 6),
     ("vz2", 8),
 )
@@ -304,6 +304,30 @@
             [jnp.concatenate([a_low, b], axis=1), jnp.concatenate([nothing, a_up], axis=1)], axis=0
         )
 
+    rest = pl.ds(0, (pairs - 1) * 16)
+
+    def wait_raw(side):
+        one = raw.at[side, pl.ds(0, 16)]
+        pltpu.make_async_copy(one, one, raw_l.at[side]).wait()
+        take(raw.at[side, rest], raw_r.at[side])
+
+    def by_rows(a, b):
+        return lax.dot_general(a, b, (((1,), (1,)), ((), ())), preferred_element_type=F32)
+
+    def prepare_columns():
+        same = (iota((chunk, chunk), 0) == iota((chunk, chunk), 1)).astype(BF)
+        here = mine * chunk + iota((chunk, chunk), 0)
+        wait_raw(1)
+        for k in range(mos):
+            there = k * chunk + iota((chunk, chunk), 1)
+            a = by_rows(same, raw[1, k * chunk : (k + 1) * chunk])
+            a_low = jnp.where(here < there, a, jnp.where(here == there, a * 0.5, 0.0))
+            right[k, :chunk, :chunk] = a_low.astype(BF)
+            right[k, :chunk, chunk:] = nothing
+            right[k, chunk:, chunk:] = jnp.where(here > there, a, 0.0).astype(BF)
+
+    prepare_columns()
+
     def occ_to_sibling(h):
         for k, step in enumerate((-1, 1, 2)):
             theirs = p_occ.at[h, lax.rem(ylo + step + YL, YL), core]
@@ -347,27 +371,10 @@
         row_part(h)
         point(3 + h)
 
-    rest = pl.ds(0, (pairs - 1) * 16)
-    for side in range(2):
-        one = raw.at[side, pl.ds(0, 16)]
-        pltpu.make_async_copy(one, one, raw_l.at[side]).wait()
-        take(raw.at[side, rest], raw_r.at[side])
-
-    def by_rows(a, b):
-        return lax.dot_general(a, b, (((1,), (1,)), ((), ())), preferred_element_type=F32)
-
-    same = (iota((chunk, chunk), 0) == iota((chunk, chunk), 1)).astype(BF)
-    here = mine * chunk + iota((chunk, chunk), 0)
+    wait_raw(0)
     for k in range(mos):
-        rows_k = slice(k * chunk, (k + 1) * chunk)
-        there = k * chunk + iota((chunk, chunk), 1)
-        a = by_rows(same, raw[1, rows_k])
-        a_low = jnp.where(here < there, a, jnp.where(here == there, a * 0.5, 0.0)).astype(BF)
-        a_up = jnp.where(here > there, a, 0.0).astype(BF)
-        b = by_rows(flip, raw[0, rows_k]).astype(BF)
-        right[k] = jnp.concatenate(
-            [jnp.concatenate([a_low, nothing], axis=1), jnp.concatenate([b, a_up], axis=1)], axis=0
-        )
+        b = by_rows(flip, raw[0, k * chunk : (k + 1) * chunk]).astype(BF)
+        right[k, chunk:, :chunk] = b
     column_sums = []
     for h in range(NP):
         column_sum = jnp.zeros((2 * chunk, ncol), F32)
@@ -400,18 +407,17 @@
         send_xo(h, 0, xo.at[m, h], to(p, other + x))
         send_xo(h, 1, xo.at[m, h], round_x(1))
         send_xo(h, 2, xo.at[m, h], round_x(-1))
+        send_xo(h, 3, xo.at[m, h], round_x(2))
 
     point(6)
-    for h in range(NP):
-        got_xo(h, 1, slot(h, base, -1))
-        send_xo(h, 3, slot(h, base, -1), round_x(1))
-    point(7)
     for h in range(NP):
         twin = xo.at[other + x, h]
         got_xo(h, 0, twin)
         send_xo(h, 4, twin, round_x(1))
         send_xo(h, 5, twin, round_x(-1))
         send_xo(h, 6, twin, round_x(2))
+        if h == 0:
+            point(7)
     point(8)
 
     take(p_vir.at[1 - core], vc_r)
@@ -427,6 +433,7 @@
 
     for h in range(NP):
         add(h, base, 0, fresh=True)
+        got_xo(h, 1, slot(h, base, -1))
         add(h, base, -1)
         add(h, other, 0)
     for h in range(NP):

time: 61.8 us -> 61.7 us (level)
  no operation moved by 1% of the time
where the time goes in v4:
time: 61.7 us; the launch traced here: 61.6 us
  Pallas kernels  59.9 us (97%)
  local copies, waits for them, and re-layouts  1.64 us (3%)
    pallas_call x1, Pallas kernels, shards(): pl.pallas_call(functools.partial(kernel, pairs, mos), out_shape=jax.Shape...  59.9 us
    unnamed x1, local copies, waits for them, and re-layouts  1.64 us

profile of v4, /device:TPU:1, one launch (start us, length us, event | category | flops | bytes accessed | tf_op | source)
XLA Modules:
  0.0 61.6 jit_solution(8848700085786427366)
XLA Ops:
  0.0 59.9 %shard_map.46 = f32[1,224,256]{2,1,0:T(8,128)} custom-call(bf16[64,16,2048]{2,1,0:T(8,128)(2,1)} %packed.1, bf16[16,64]{1,0:T(8,128)(2,1)} %bitcast.3, bf16[32,32]{1,0:T(8,128)(2,1)} %occ_in.1, bf16[32,224]{1,0:T(8,128)(2,1)} %vir_in.1), custom_call_target="tpu_custom_call" | custom-call | tf_op jit(solution)/shard_map/pallas_call | solution.py:489
  59.9 1.6 %copy.6 = f32[1,256,224]{1,2,0:T(8,128)} copy(f32[1,256,224]{1,2,0:T(8,128)} %bitcast.2) | data formatting | bytes 458752

commit v5 on v4

--- a/solution.py
+++ b/solution.py
@@ -449,7 +449,7 @@
     for h in range(NP):
         got_xo(h, 6, slot(h, other, 2))
         add(h, other, 2)
-    out[0] = jnp.concatenate([acc[h, :nvir] for h in range(NP)], axis=1)
+        out[0, :, h * ncol : (h + 1) * ncol] = acc[h, :nvir]
 
     take(part.at[pl.ds(0, mos - 1)], part_s)
     for h in range(NP):

time: 61.7 us -> 61.7 us (level)
  no operation moved by 1% of the time
where the time goes in v5:
time: 61.7 us; the launch traced here: 61.6 us
  Pallas kernels  59.9 us (97%)
  local copies, waits for them, and re-layouts  1.64 us (3%)
    pallas_call x1, Pallas kernels, shards(): pl.pallas_call(functools.partial(kernel, pairs, mos), out_shape=jax.Shape...  59.9 us
    unnamed x1, local copies, waits for them, and re-layouts  1.64 us

profile of v5, /device:TPU:1, one launch (start us, length us, event | category | flops | bytes accessed | tf_op | source)
XLA Modules:
  0.0 61.6 jit_solution(13772990466417634172)
XLA Ops:
  0.0 59.9 %shard_map.46 = f32[1,224,256]{2,1,0:T(8,128)} custom-call(bf16[64,16,2048]{2,1,0:T(8,128)(2,1)} %packed.1, bf16[16,64]{1,0:T(8,128)(2,1)} %bitcast.3, bf16[32,32]{1,0:T(8,128)(2,1)} %occ_in.1, bf16[32,224]{1,0:T(8,128)(2,1)} %vir_in.1), custom_call_target="tpu_custom_call" | custom-call | tf_op jit(solution)/shard_map/pallas_call | solution.py:489
  59.9 1.6 %copy.6 = f32[1,256,224]{1,2,0:T(8,128)} copy(f32[1,256,224]{1,2,0:T(8,128)} %bitcast.2) | data formatting | bytes 458752
